TPU v7x, 32 devices: a whole 2x2x4 slice. The times are simulated.
32 devices in a mesh: member: 2 (over x), grid: 16 (over z, y, core).
Axes of the slice: x: 2, y: 2, z: 4, core: 2. Of those that a mesh axis runs over, the one named last changes fastest.
Arguments:
- latent: bfloat16 [16, 49152, 512], P('member', 'grid'), may hold values from -6 to 6
- weight_in: bfloat16 [512, 512], replicated, may hold values from -0.25 to 0.25
- bias_in: float32 [512], replicated, may hold values from -3 to 3
- weight_out: bfloat16 [512, 8], replicated, may hold values from -0.25 to 0.25
- bias_out: float32 [8], replicated, may hold values from -3 to 3
- member_rank: int32 [16, 8, 49152], P('member', None, 'grid'), may hold values from 0 to 31, as said below
- target_level: int32 [8, 49152], P(None, 'grid'), may hold values from 0 to 32
- target_jitter: float32 [8, 49152], P(None, 'grid'), may hold values from -1 to 1
- var_weight: float32 [8], replicated, may hold values from 0.25 to 4
Outputs:
- grad_weight_in: float32 [512, 512], P('grid')
- grad_bias_in: float32 [512], replicated
- grad_weight_out: float32 [512, 8], replicated
- grad_bias_out: float32 [8], replicated
Inputs may be any that keep to these rules, and one draw needn't show every extreme that they name: `member_rank`: at each variable and cell the 16 members' offsets are distinct whole numbers.
All inputs are finite; a program needn't handle non-finite values.
Results may differ from a plain program's by a relative error of at most 0.00069.
Values sent between devices are 32-bit elements; how exact they have to be, the bound alone decides.
A program may use at most 384 MiB of HBM per device.

v0:
```python
import math

import jax
import jax.numpy as jnp
from jax import lax
from jax.sharding import PartitionSpec as P

LONS = 1440


north_row = 200.0
mean_weight = 0.05
smooth_square = 0.01


def area_weights(first_cell, count):
    global_cell = first_cell + jnp.arange(count, dtype=jnp.int32)
    lat_row = (global_cell // LONS).astype(jnp.float32)
    latitude = (90.0 - 0.25 * (north_row + lat_row)) * (math.pi / 180.0)
    return jnp.cos(latitude)


def soft_sign(values):
    return values / jnp.sqrt(values * values + smooth_square)


def crps_slopes(fields, target, area, var_weight):
    members = fields.shape[0]
    center = jnp.mean(fields, axis=0)
    pair_sum = jnp.sum(soft_sign(fields[:, None] - fields[None, :]), axis=1)
    weights = var_weight[:, None] * area[None, :]
    return weights[None] * (
        soft_sign(fields - target[None])
        - pair_sum / (members - 1)
        + 2.0 * mean_weight * (center - target)[None]
    )


def gelu_tanh(values):
    return jax.nn.gelu(values, approximate=True)


def shards(
    latent,
    weight_in,
    bias_in,
    weight_out,
    bias_out,
    member_rank,
    target_level,
    target_jitter,
    var_weight,
):
    mem_dev, cell_count, in_width = latent.shape
    member_groups = lax.axis_size("member")
    members = mem_dev * member_groups
    all_cells = cell_count * lax.axis_size("grid")
    loss_scale = 2.0 / math.sqrt(all_cells * members)
    flat_rows = latent.reshape(mem_dev * cell_count, in_width)
    preact = jnp.dot(flat_rows, weight_in, preferred_element_type=jnp.float32) + bias_in
    hidden = gelu_tanh(preact).astype(jnp.bfloat16)
    hidden_cube = hidden.reshape(mem_dev, cell_count, -1)
    outputs = (
        jnp.einsum("mch,hv->mvc", hidden_cube, weight_out, preferred_element_type=jnp.float32)
        + bias_out[None, :, None]
    )
    squash = jnp.tanh(outputs)
    fields = 0.1 * member_rank.astype(jnp.float32) + squash
    target = 0.1 * target_level.astype(jnp.float32) + 0.5 * target_jitter - 0.5
    first_cell = lax.axis_index("grid") * cell_count
    area = area_weights(first_cell, cell_count)
    pooled = lax.all_to_all(fields, "member", split_axis=2, concat_axis=0, tiled=True)
    part_cells = cell_count // member_groups
    offset = lax.axis_index("member") * part_cells
    part_target = lax.dynamic_slice_in_dim(target, offset, part_cells, 1)
    part_area = lax.dynamic_slice_in_dim(area, offset, part_cells, 0)
    pooled_slopes = crps_slopes(pooled, part_target, part_area, var_weight)
    slopes = lax.all_to_all(pooled_slopes, "member", split_axis=0, concat_axis=2, tiled=True)
    out_grad = slopes * (1.0 - squash * squash) * loss_scale
    out_grad_b = out_grad.astype(jnp.bfloat16)
    hid_grad = jnp.einsum(
        "mvc,hv->mch", out_grad_b, weight_out, preferred_element_type=jnp.float32
    ).reshape(mem_dev * cell_count, -1)
    gelu_out, pull_back = jax.vjp(gelu_tanh, preact)
    pre_grad = pull_back(hid_grad)[0]
    pre_grad_b = pre_grad.astype(jnp.bfloat16)
    local_b_in = jnp.sum(pre_grad, axis=0)
    local_w_out = jnp.einsum(
        "mch,mvc->hv", hidden_cube, out_grad_b, preferred_element_type=jnp.float32
    )
    local_b_out = jnp.sum(out_grad, axis=(0, 2))
    grad_b_in, grad_w_out, grad_b_out = lax.psum(
        (local_b_in, local_w_out, local_b_out), ("member", "grid")
    )
    contract = (((0,), (0,)), ((), ()))
    local_grad = lax.dot_general(
        flat_rows, pre_grad_b, contract, preferred_element_type=jnp.float32
    )
    summed = lax.psum(local_grad, "member")
    grad_shard = lax.psum_scatter(summed, "grid", scatter_dimension=0, tiled=True)
    return (grad_shard, grad_b_in, grad_w_out, grad_b_out)


def solution(mesh):
    in_specs = (
        P("member", "grid", None),
        P(),
        P(),
        P(),
        P(),
        P("member", None, "grid"),
        P(None, "grid"),
        P(None, "grid"),
        P(),
    )
    out_specs = (P("grid", None), P(), P(), P())
    return jax.shard_map(shards, mesh=mesh, in_specs=in_specs, out_specs=out_specs, check_vma=False)
```

profile of v0, /device:TPU:0, one launch (start us, length us, event | category | flops | bytes accessed | tf_op | source)
XLA Modules:
  0.0 347.5 jit_solution(4420442431986162565)
XLA Ops:
  7.2 0.0 copy-start
  7.2 1.0 copy-done
  8.2 0.0 copy-start.2
  8.2 0.0 copy-start.3
  8.2 0.0 copy-start.6
  8.2 38.5 %multiply_convert_fusion = (bf16[24576,512]{1,0:T(8,128)(2,1)}, f32[24576,512]{1,0:T(8,128)}) fusion(f32[512]{0:T(512)} %param.11, bf16[24576,512]{1,0:T(8,128)(2,1)} %bitcast.57, bf16[512,512]{1,0:T(8,128)(2,1)S(1)} %copy-done), kind=kOutput, calls=%fused_computation.13 | convolution fusion | flops 13010731008 | bytes 101189632 | tf_op jit(solution)/shard_map/dot_general | solution.py:60
  46.7 0.0 copy-start.4
  46.7 0.0 copy-start.5
  46.7 0.0 copy-start.8
  46.7 0.0 copy-done.2
  46.8 0.0 copy-done.3
  46.8 0.0 copy-done.6
  46.8 11.6 %multiply_add_fusion = (f32[8,8,3072]{2,1,0:T(8,128)S(1)}, f32[8,8,3072]{2,1,0:T(8,128)S(1)}) fusion(s32[8,8,3072]{2,1,0:T(8,128)S(1)} %copy-done.2, f32[8]{0:T(128)S(1)} %copy-done.6, bf16[8,3072,512]{2,1,0:T(8,128)(2,1)} %bitcast.49, bf16[512,8]{0,1:T(8,128)(2,1)S(1)} %copy-done.3), kind=kOutput, calls=%fused_computation.28 | convolution fusion | flops 202113024 | bytes 27533344 | tf_op jit(solution)/shard_map/mch,hv->mvc/dot_general | solution.py:64
  58.4 6.6 %copy.25 = f32[8,8,3072]{1,0,2:T(8,128)} copy(f32[8,8,3072]{2,1,0:T(8,128)S(1)} %get-tuple-element.35) | data formatting | bytes 1572864 | tf_op jit(solution)/shard_map/add | solution.py:68
  65.0 13.7 %reshape.60 = f32[2,1,98304]{2,1,0:T(1,128)} reshape(f32[3072,8,8]{2,1,0:T(8,128)} %bitcast.51) | data formatting | bytes 1572864
  78.7 4.5 %all-to-all-start = ((f32[2,1,98304]{2,1,0:T(1,128)}), f32[2,1,98304]{2,1,0:T(1,128)S(1)}, u32[]{:S(2)}, u32[]{:S(2)}) async-start(f32[2,1,98304]{2,1,0:T(1,128)} %reshape.60), calls=%async_computation | async-start | bytes 1572864 | tf_op jit(solution)/shard_map/all_to_all | solution.py:72
  83.1 0.0 reduce-scatter.4.cloned.1.call-start
  83.2 0.1 fusion.29
  83.3 11.4 %all-to-all-done = f32[2,1,98304]{2,1,0:T(1,128)S(1)} async-done(((f32[2,1,98304]{2,1,0:T(1,128)}), f32[2,1,98304]{2,1,0:T(1,128)S(1)}, u32[]{:S(2)}, u32[]{:S(2)}) %all-to-all-start) | async-done | bytes 786464 | tf_op jit(solution)/shard_map/all_to_all | solution.py:72
  94.7 0.5 broadcast.71
  95.2 3.1 reduce.1
  98.4 0.0 copy-start.7
  98.4 11.7 %reshape.61 = f32[3072,8,8]{2,1,0:T(8,128)} reshape(f32[2,98304]{1,0:T(2,128)S(1)} %reduce.1) | data formatting | bytes 1572864
  110.1 7.5 %copy.30 = f32[8,8,2,1536]{3,2,1,0:T(2,128)S(1)} copy(f32[8,8,2,1536]{1,0,3,2:T(8,128)} %bitcast.52) | data formatting | bytes 1572864 | tf_op jit(solution)/shard_map/all_to_all | solution.py:72
  117.6 0.2 bitcast_reduce_fusion
  117.9 0.2 copy.27
  118.0 2.4 fusion.13
  120.5 0.0 copy-done.4
  120.5 0.0 copy-done.5
  120.5 0.0 copy-done.8
  120.5 0.1 subtract_multiply_fusion.2
  120.6 0.2 add_multiply_fusion
  120.8 22.1 %all_to_all.36 = f32[16,8,1536]{2,1,0:T(8,128)S(1)} all-to-all(f32[16,8,1536]{2,1,0:T(8,128)S(1)} %add_multiply_fusion), channel_id=1, replica_groups=mesh['member'=2,'grid'=16] {'member'}, dimensions={0} | all-to-all | bytes 1572864 | tf_op jit(solution)/shard_map/all_to_all | solution.py:78
  142.9 0.1 copy.28
  143.0 0.3 fusion.19
  143.3 19.3 %fusion.30 = f32[8,3072,512]{2,1,0:T(8,128)} fusion(bf16[8,8,3072]{2,1,0:T(8,128)(2,1)S(1)} %get-tuple-element.32, bf16[512,8]{0,1:T(8,128)(2,1)S(1)} %copy-done.3), kind=kOutput, calls=%fused_computation.49 | convolution fusion | flops 201326592 | bytes 50733056 | tf_op jit(solution)/shard_map/mvc,hv->mch/dot_general | solution.py:81
  162.6 0.0 copy-done.7
  162.6 42.8 %fusion.33 = (f32[512]{0:T(512)S(1)}, bf16[24576,512]{1,0:T(8,128)(2,1)}) fusion(f32[24576,512]{1,0:T(8,128)} %get-tuple-element.34, f32[512]{0:T(512)S(1)} %copy-done.7, f32[8,3072,512]{2,1,0:T(8,128)} %fusion.30), kind=kLoop, calls=%fused_computation.53 | loop fusion | flops 276823552 | bytes 125833216 | tf_op jit(solution)/shard_map/reduce_sum | solution.py:87
  205.5 0.0 copy-start.1
  205.5 22.1 %fusion.16 = f32[512,512]{0,1:T(8,128)S(1)} fusion(bf16[24576,512]{1,0:T(8,128)(2,1)} %bitcast.58, bf16[24576,512]{1,0:T(8,128)(2,1)} %get-tuple-element.28), kind=kOutput, calls=%fused_computation.24 | convolution fusion | flops 12884901888 | bytes 51380224 | tf_op jit(solution)/shard_map/dot_general | solution.py:96
  227.5 1.3 copy.31
  228.9 0.0 reduce-scatter.4.cloned.1.call-update
  228.9 0.0 all-reduce.3.cloned.1.call-start
  228.9 57.8 %reduce-scatter.4.cloned.1.call-done = f32[32,512]{1,0:T(8,128)} async-done(((f32[512,512]{1,0:T(8,128)}), f32[32,512]{1,0:T(8,128)}) %reduce-scatter.4.cloned.1.call-update) | async-done | bytes 65552
  286.7 1.7 copy.32
  288.4 0.0 all-reduce.3.cloned.1.call-update
  288.4 10.0 %convolution_bitcast_fusion = f32[512,8]{0,1:T(8,128)S(1)} fusion(bf16[8,3072,512]{2,1,0:T(8,128)(2,1)} %bitcast.50, bf16[8,8,3072]{2,1,0:T(8,128)(2,1)S(1)} %get-tuple-element.32), kind=kOutput, calls=%fused_computation.25 | convolution fusion | flops 201326592 | bytes 25575424 | tf_op jit(solution)/shard_map/mch,mvc->hv/dot_general | solution.py:88
  298.4 40.4 %all-reduce = (f32[512]{0:T(512)}, f32[512,8]{0,1:T(8,128)}, f32[8]{0:T(128)}) all-reduce(f32[512]{0:T(512)S(1)} %get-tuple-element.27, f32[512,8]{0,1:T(8,128)S(1)} %convolution_bitcast_fusion, f32[8]{0:T(128)S(1)} %get-tuple-element.31), channel_id=1, replica_groups=mesh['member'=2,'grid'=16] {'member','grid'}, use_global_device_ids=true, to_apply=%region_5.6 | all-reduce | flops 4616 | bytes 36928 | tf_op jit(solution)/shard_map/psum | solution.py:92
  338.7 0.0 all-reduce.3.cloned.1.call-done
  338.7 1.7 copy.29
  340.4 0.0 copy-done.1
  (1 shorter events, 0.0 us)
Async XLA Ops:
  7.2 1.1 copy-start
  8.2 38.5 %copy-start.2 = (s32[8,8,3072]{2,1,0:T(8,128)S(1)}, s32[8,8,3072]{2,1,0:T(8,128)}, u32[]{:S(2)}) copy-start(s32[8,8,3072]{2,1,0:T(8,128)} %param.14) | copy-start | bytes 2359300
  8.2 38.5 %copy-start.3 = (bf16[512,8]{0,1:T(8,128)(2,1)S(1)}, bf16[512,8]{0,1:T(8,128)(2,1)}, u32[]{:S(2)}) copy-start(bf16[512,8]{0,1:T(8,128)(2,1)} %param.12) | copy-start | bytes 24580
  8.2 38.6 %copy-start.6 = (f32[8]{0:T(128)S(1)}, f32[8]{0:T(128)}, u32[]{:S(2)}) copy-start(f32[8]{0:T(128)} %param.13) | copy-start | bytes 100
  46.7 73.7 %copy-start.4 = (f32[8,3072]{1,0:T(8,128)S(1)}, f32[8,3072]{1,0:T(8,128)}, u32[]{:S(2)}) copy-start(f32[8,3072]{1,0:T(8,128)} %param.16) | copy-start | bytes 294916
  46.7 73.7 %copy-start.5 = (s32[8,3072]{1,0:T(8,128)S(1)}, s32[8,3072]{1,0:T(8,128)}, u32[]{:S(2)}) copy-start(s32[8,3072]{1,0:T(8,128)} %param.15) | copy-start | bytes 294916
  46.7 73.7 %copy-start.8 = (f32[8]{0:T(128)S(1)}, f32[8]{0:T(128)}, u32[]{:S(2)}) copy-start(f32[8]{0:T(128)} %param.17) | copy-start | bytes 100
  78.7 16.0 %all-to-all-start = ((f32[2,1,98304]{2,1,0:T(1,128)}), f32[2,1,98304]{2,1,0:T(1,128)S(1)}, u32[]{:S(2)}, u32[]{:S(2)}) async-start(f32[2,1,98304]{2,1,0:T(1,128)} %reshape.60), calls=%async_computation | async-start | bytes 1572864 | tf_op jit(solution)/shard_map/all_to_all | solution.py:72
  83.1 203.6 %reduce-scatter.4.cloned.1.call-start = ((), (), s32[]{:S(2)}) async-start(), calls=%async_computation.4 | async-start | bytes 1114112
  98.4 64.3 %copy-start.7 = (f32[512]{0:T(512)S(1)}, f32[512]{0:T(512)}, u32[]{:S(2)}) copy-start(f32[512]{0:T(512)} %param.11) | copy-start | bytes 6148
  205.5 135.0 %copy-start.1 = (bf16[512,512]{1,0:T(8,128)(2,1)S(1)}, bf16[512,512]{1,0:T(8,128)(2,1)}, u32[]{:S(2)}) copy-start(bf16[512,512]{1,0:T(8,128)(2,1)} %param.10) | copy-start | bytes 1572868
  228.9 109.9 %all-reduce.3.cloned.1.call-start = ((), (), s32[]{:S(2)}) async-start(), calls=%async_computation.3 | async-start | bytes 524288 | tf_op jit(solution)/shard_map/psum | solution.py:99
Sparse Core Ops, SparseCore 0:
  229.0 57.6 reduce-scatter.3
  289.1 22.2 all-reduce.2
where the time goes:
time: 352 us; the launch traced here: 347 us
  matrix products  101 us (29%)
  waiting for transfers between devices  69.2 us (20%)
  blocking collectives  62.4 us (18%)
  other arithmetic  49.4 us (14%)
  local copies, waits for them, and re-layouts  46 us (13%)
  between operations  14.4 us (4%)
  starting transfers between devices  4.5 us (1%)
    unnamed x3, waiting for transfers between devices  57.8 us
    reduce_sum x1, other arithmetic, shards(): local_b_in = jnp.sum(pre_grad, axis=0)  42.8 us
    psum x1, blocking collectives, shards(): lax.psum((local_b_in, local_w_out, local_b_out), ('member', 'grid'))  40.4 us
    dot_general x1, matrix products, shards(): jnp.dot(flat_rows, weight_in, preferred_element_type=jnp.float32) + bias_in  38.5 us
    unnamed x23, local copies, waits for them, and re-layouts  31.2 us
    all_to_all x1, blocking collectives, shards(): lax.all_to_all(pooled_slopes, 'member', split_axis=0, concat_axis=2, tile...  22.1 us
    dot_general x1, matrix products, shards(): lax.dot_general(flat_rows, pre_grad_b, contract, preferred_element_type=j...  22.1 us
    dot_general x1, matrix products, shards(): jnp.einsum('mvc,hv->mch', out_grad_b, weight_out, preferred_element_type=...  19.3 us
  transfers between devices with their start and end apart: 3, of which 2 were waited for; matrix products, arithmetic and copies ran while one was open for 3% of the time, Pallas kernels for 0%

commit v1 on v0

v1 whole, which is shorter than its diff:
```python
import functools
import math

import jax
import jax.numpy as jnp
from jax import lax
from jax.experimental import pallas as pl
from jax.experimental.pallas import tpu as pltpu
from jax.sharding import PartitionSpec as P

LONS = 1440
LAG = 2
TILE = 128
CHUNK_ROWS = 256
SUB_ROWS = 32

north_row = 200.0
mean_weight = 0.05
smooth_square = 0.01
root_two_pi = math.sqrt(2.0 / math.pi)
cube_coef = 0.044715


def area_weights(first_cell, count):
    global_cell = first_cell + jnp.arange(count, dtype=jnp.int32)
    lat_row = (global_cell // LONS).astype(jnp.float32)
    latitude = (90.0 - 0.25 * (north_row + lat_row)) * (math.pi / 180.0)
    return jnp.cos(latitude)


def soft_sign(values):
    return values * lax.rsqrt(values * values + smooth_square)


def fused_kernel(
    groups,
    tiles,
    lat_ref,
    late_ref,
    w_in_ref,
    b_in_ref,
    w_out_t_ref,
    b_out_ref,
    rank_ref,
    level_ref,
    jitter_ref,
    weight_ref,
    grad_ref,
    small_ref,
    hid_buf,
    slope_buf,
    pre_buf,
    field_buf,
    squash_buf,
    recv_buf,
    bias_acc,
    out_acc,
    send_sem,
    recv_sem,
):
    step = pl.program_id(0)
    me = lax.axis_index("member")
    mem_dev, tile, in_width = lat_ref.shape
    width = w_in_ref.shape[1]
    nvars = w_out_t_ref.shape[0]
    rows = mem_dev * tile
    members = mem_dev * groups
    mem_chunk = max(1, CHUNK_ROWS // tile)
    chunk_rows = mem_chunk * tile

    def copies(index):
        made = []
        for hop in range(1, groups):
            made.append(
                pltpu.make_async_remote_copy(
                    src_ref=field_buf.at[index],
                    dst_ref=recv_buf.at[hop - 1, index],
                    send_sem=send_sem.at[hop - 1, index],
                    recv_sem=recv_sem.at[hop - 1, index],
                    device_id={"member": lax.rem(me + hop, groups)},
                    device_id_type=pl.DeviceIdType.MESH,
                )
            )
        return made

    def loss_part(index):
        own = [field_buf[index, pl.ds(m * nvars, nvars), :] for m in range(mem_dev)]
        other = [
            recv_buf[g, index, pl.ds(m * nvars, nvars), :]
            for g in range(groups - 1)
            for m in range(mem_dev)
        ]
        target = 0.1 * level_ref[...].astype(jnp.float32) + 0.5 * jitter_ref[...] - 0.5
        center = own[0]
        for value in own[1:] + other:
            center = center + value
        pull = (2.0 * mean_weight) * (center * (1.0 / members) - target)
        weight = weight_ref[...]
        pair = [jnp.zeros_like(target) for _ in range(mem_dev)]
        for a in range(mem_dev):
            for b in range(a + 1, mem_dev):
                value = soft_sign(own[a] - own[b])
                pair[a] = pair[a] + value
                pair[b] = pair[b] - value
            for value in other:
                pair[a] = pair[a] + soft_sign(own[a] - value)
        grads = []
        for m in range(mem_dev):
            squash = squash_buf[index, pl.ds(m * nvars, nvars), :]
            slope = weight * (soft_sign(own[m] - target) - pair[m] * (1.0 / (members - 1)) + pull)
            grads.append(slope * (1.0 - squash * squash))
        total = grads[0]
        for value in grads[1:]:
            total = total + value
        out_acc[...] += total
        return jnp.concatenate(grads, axis=1)

    def forward_chunk(index, slot, chunk):
        first = chunk * mem_chunk
        block = lat_ref[pl.ds(first, mem_chunk)].reshape(chunk_rows, in_width)
        raw = jnp.dot(block, w_in_ref[...], preferred_element_type=jnp.float32)
        bias = b_in_ref[...]
        for sub in range(0, chunk_rows, SUB_ROWS):
            pre = raw[sub : sub + SUB_ROWS] + bias
            square = pre * pre
            arg = pre * (root_two_pi + (root_two_pi * cube_coef) * square)
            gate = 0.5 + 0.5 * jnp.tanh(arg)
            hid = pre * gate
            rate = (2.0 * root_two_pi) + (6.0 * root_two_pi * cube_coef) * square
            place = pl.ds(chunk * chunk_rows + sub, SUB_ROWS)
            hid_buf[slot, place, :] = hid.astype(jnp.bfloat16)
            slope_buf[slot, place, :] = gate + hid * (1.0 - gate) * rate
        hid_block = hid_buf[slot, pl.ds(chunk * chunk_rows, chunk_rows), :]
        outs = lax.dot_general(
            w_out_t_ref[...], hid_block, (((1,), (1,)), ((), ())), preferred_element_type=jnp.float32
        )
        squash = jnp.tanh(outs + b_out_ref[...])
        for m in range(mem_chunk):
            part = squash[:, m * tile : (m + 1) * tile]
            place = pl.ds((first + m) * nvars, nvars)
            squash_buf[index, place, :] = part
            field_buf[index, place, :] = 0.1 * rank_ref[first + m].astype(jnp.float32) + part

    def backward_chunk(slot, chunk, grads_rows):
        base = chunk * chunk_rows
        hid_grad = jnp.dot(
            grads_rows[base : base + chunk_rows], w_out_t_ref[...], preferred_element_type=jnp.float32
        )
        total = jnp.zeros((8, width), jnp.float32)
        for sub in range(0, chunk_rows, SUB_ROWS):
            place = pl.ds(base + sub, SUB_ROWS)
            pre_grad = hid_grad[sub : sub + SUB_ROWS] * slope_buf[slot, place, :]
            pre_buf[place, :] = pre_grad.astype(jnp.bfloat16)
            total = total + jnp.sum(pre_grad.reshape(SUB_ROWS // 8, 8, width), axis=0)
        bias_acc[...] += total

    def run(do_forward, do_backward):
        late = step - LAG
        if do_backward:
            for copy in copies(late):
                copy.wait()
            late_slot = lax.rem(late, LAG + 1)
            grads = loss_part(late)
            grads_b = grads.astype(jnp.bfloat16)
            grads_rows = jnp.transpose(grads, (1, 0)).astype(jnp.bfloat16)
        slot = lax.rem(step, LAG + 1)
        for chunk in range(rows // chunk_rows):
            if do_backward:
                backward_chunk(late_slot, chunk, grads_rows)
            if do_forward:
                forward_chunk(step, slot, chunk)
        if do_forward:
            for copy in copies(step):
                copy.start()
        if do_backward:
            small_ref[0:nvars, :] += jnp.dot(
                grads_b, hid_buf[late_slot], preferred_element_type=jnp.float32
            )
            grad_ref[...] += lax.dot_general(
                late_ref[...].reshape(rows, in_width),
                pre_buf[...],
                (((0,), (0,)), ((), ())),
                preferred_element_type=jnp.float32,
            )

    @pl.when(step == 0)
    def _():
        barrier = pltpu.get_barrier_semaphore()
        for hop in range(1, groups):
            pl.semaphore_signal(
                barrier,
                inc=1,
                device_id={"member": lax.rem(me + hop, groups)},
                device_id_type=pl.DeviceIdType.MESH,
            )
        pl.semaphore_wait(barrier, groups - 1)
        grad_ref[...] = jnp.zeros_like(grad_ref)
        small_ref[...] = jnp.zeros_like(small_ref)
        bias_acc[...] = jnp.zeros_like(bias_acc)
        out_acc[...] = jnp.zeros_like(out_acc)

    @pl.when(step < LAG)
    def _():
        run(True, False)

    @pl.when(jnp.logical_and(step >= LAG, step < tiles))
    def _():
        run(True, True)

    @pl.when(step >= tiles)
    def _():
        run(False, True)

    @pl.when(step == tiles + LAG - 1)
    def _():
        small_ref[nvars : nvars + 8, :] = bias_acc[...]
        small_ref[nvars + 8 : 2 * nvars + 8, :] = jnp.broadcast_to(
            jnp.sum(out_acc[...], axis=1, keepdims=True), (nvars, width)
        )


def shards(
    latent,
    weight_in,
    bias_in,
    weight_out,
    bias_out,
    member_rank,
    target_level,
    target_jitter,
    var_weight,
):
    mem_dev, cell_count, in_width = latent.shape
    width = weight_in.shape[1]
    nvars = weight_out.shape[1]
    groups = lax.axis_size("member")
    members = mem_dev * groups
    all_cells = cell_count * lax.axis_size("grid")
    loss_scale = 2.0 / math.sqrt(all_cells * members)
    tiles = cell_count // TILE
    rows = mem_dev * TILE
    first_cell = lax.axis_index("grid") * cell_count
    area = area_weights(first_cell, cell_count)
    weights = (var_weight[:, None] * area[None, :]) * loss_scale

    def now(step):
        return jnp.minimum(step, tiles - 1)

    def late(step):
        return jnp.maximum(step - LAG, 0)

    def whole(*shape):
        return pl.BlockSpec(shape, lambda step: (0,) * len(shape))

    cell_spec = pl.BlockSpec((nvars, TILE), lambda step: (0, late(step)))
    local_grad, small = pl.pallas_call(
        functools.partial(fused_kernel, groups, tiles),
        grid=(tiles + LAG,),
        in_specs=[
            pl.BlockSpec((mem_dev, TILE, in_width), lambda step: (0, now(step), 0)),
            pl.BlockSpec((mem_dev, TILE, in_width), lambda step: (0, late(step), 0)),
            whole(in_width, width),
            whole(1, width),
            whole(nvars, width),
            whole(nvars, 1),
            pl.BlockSpec((mem_dev, nvars, TILE), lambda step: (0, 0, now(step))),
            cell_spec,
            cell_spec,
            cell_spec,
        ],
        out_specs=[whole(in_width, width), whole(2 * nvars + 8, width)],
        out_shape=[
            jax.ShapeDtypeStruct((in_width, width), jnp.float32),
            jax.ShapeDtypeStruct((2 * nvars + 8, width), jnp.float32),
        ],
        scratch_shapes=[
            pltpu.VMEM((LAG + 1, rows, width), jnp.bfloat16),
            pltpu.VMEM((LAG + 1, rows, width), jnp.float32),
            pltpu.VMEM((rows, width), jnp.bfloat16),
            pltpu.VMEM((tiles, mem_dev * nvars, TILE), jnp.float32),
            pltpu.VMEM((tiles, mem_dev * nvars, TILE), jnp.float32),
            pltpu.VMEM((groups - 1, tiles, mem_dev * nvars, TILE), jnp.float32),
            pltpu.VMEM((8, width), jnp.float32),
            pltpu.VMEM((nvars, TILE), jnp.float32),
            pltpu.SemaphoreType.DMA((groups - 1, tiles)),
            pltpu.SemaphoreType.DMA((groups - 1, tiles)),
        ],
        compiler_params=pltpu.CompilerParams(
            collective_id=0,
            has_side_effects=True,
            vmem_limit_bytes=56 * 1024 * 1024,
            dimension_semantics=("arbitrary",),
        ),
    )(
        latent,
        latent,
        weight_in,
        bias_in.reshape(1, -1),
        weight_out.T,
        bias_out.reshape(-1, 1),
        member_rank,
        target_level,
        target_jitter,
        weights,
    )
    total = lax.psum(small, ("member", "grid"))
    grad_w_out = total[:nvars].T
    grad_b_in = jnp.sum(total[nvars : nvars + 8], axis=0)
    grad_b_out = total[nvars + 8 :, 0]
    summed = lax.psum(local_grad, "member")
    grad_shard = lax.psum_scatter(summed, "grid", scatter_dimension=0, tiled=True)
    return (grad_shard, grad_b_in, grad_w_out, grad_b_out)


def solution(mesh):
    in_specs = (
        P("member", "grid", None),
        P(),
        P(),
        P(),
        P(),
        P("member", None, "grid"),
        P(None, "grid"),
        P(None, "grid"),
        P(),
    )
    out_specs = (P("grid", None), P(), P(), P())
    return jax.shard_map(shards, mesh=mesh, in_specs=in_specs, out_specs=out_specs, check_vma=False)
```

time: 352 us -> 185 us (0.53); the launches traced: 347 us -> 184 us
  matrix products: 101 us -> 0 us
  Pallas kernels: 0 us -> 85.9 us
  other arithmetic: 49.4 us -> 2.64 us
  local copies, waits for them, and re-layouts: 46 us -> 3.42 us
  waiting for transfers between devices: 69.2 us -> 37.7 us
  blocking collectives: 62.4 us -> 40.4 us
  starting transfers between devices: 4.5 us -> 0.08 us
    dot_general x5 -> x0, matrix products: 101 us -> none  [the longest x1 38.5 us: shards(): jnp.dot(flat_rows, weight_in, preferred_element_type=jnp.float32) + bias_in]
    pallas_call x0 -> x1, Pallas kernels: none -> 85.9 us  [shards(): pl.pallas_call(functools.partial(fused_kernel, groups, tiles), grid=(tile...]
    unnamed x3 -> x2, waiting for transfers between devices: 57.8 us -> 0.03 us
    reduce_sum x4 -> x0, other arithmetic: 45.8 us -> none  [the longest x1 42.8 us: shards(): local_b_in = jnp.sum(pre_grad, axis=0)]
    unnamed x23 -> x1, local copies, waits for them, and re-layouts: 31.2 us -> 1.47 us
    all_to_all x1 -> x0, blocking collectives: 22.1 us -> none  [shards(): lax.all_to_all(pooled_slopes, 'member', split_axis=0, concat_axis=2, tile...]
    psum x1, waiting for transfers between devices: 0.01 us -> 21.5 us  [shards(): summed = lax.psum(local_grad, 'member')]
    reduce_scatter x0 -> x1, waiting for transfers between devices: none -> 16.2 us  [shards(): lax.psum_scatter(summed, 'grid', scatter_dimension=0, tiled=True)]
  transfers between devices with their start and end apart: 3 -> 2, of which waited for: 2 -> 2; matrix products, arithmetic and copies ran while one was open for 3% -> 1% of each run, Pallas kernels for 0% -> 0%
where the time goes in v1:
time: 185 us; the launch traced here: 184 us
  Pallas kernels  85.9 us (46%)
  blocking collectives  40.4 us (22%)
  waiting for transfers between devices  37.7 us (20%)
  between operations  14.1 us (8%)
  local copies, waits for them, and re-layouts  3.42 us (2%)
  other arithmetic  2.64 us (1%)
    pallas_call x1, Pallas kernels, shards(): pl.pallas_call(functools.partial(fused_kernel, groups, tiles), grid=(tile...  85.9 us
    psum x1, blocking collectives, shards(): total = lax.psum(small, ('member', 'grid'))  40.4 us
    psum x1, waiting for transfers between devices, shards(): summed = lax.psum(local_grad, 'member')  21.5 us
    reduce_scatter x1, waiting for transfers between devices, shards(): lax.psum_scatter(summed, 'grid', scatter_dimension=0, tiled=True)  16.2 us
  transfers between devices with their start and end apart: 2, of which 2 were waited for; matrix products, arithmetic and copies ran while one was open for 1% of the time, Pallas kernels for 0%

profile of v1, /device:TPU:0, one launch (start us, length us, event | category | flops | bytes accessed | tf_op | source)
XLA Modules:
  0.0 184.2 jit_solution(16743766566590172265)
XLA Ops:
  7.2 0.0 reduce-scatter.2.cloned.1.call-start
  7.2 1.3 copy.14.b_out_ref
  8.5 0.1 fusion.5
  8.6 1.4 multiply_multiply_fusion.weight_ref
  10.0 85.9 %shard_map.120 = (f32[512,512]{1,0:T(8,128)}, f32[24,512]{1,0:T(8,128)}) custom-call(bf16[8,3072,512]{2,1,0:T(8,128)(2,1)} %late_ref.1, bf16[8,3072,512]{2,1,0:T(8,128)(2,1)} %late_ref.1, bf16[512,512]{1,0:T(8,128)(2,1)} %w_in_ref.1, f32[1,512]{1,0:T(1,128)} %bitcast.6, bf16[8,512]{1,0:T(8,128)(2,1)} %bitcast.5, f32[8,1]{1,0:T(8,128)} %copy.14.b_out_ref, ...), custom_call_target="tpu_custom_call" | custom-call | tf_op jit(solution)/shard_map/pallas_call | solution.py:256
  95.9 0.0 reduce-scatter.2.cloned.1.call-update
  95.9 0.0 all-reduce.2.cloned.1.call-start
  96.0 40.4 %psum.15 = f32[24,512]{1,0:T(8,128)S(1)} all-reduce(f32[24,512]{1,0:T(8,128)} %get-tuple-element.7), channel_id=1, replica_groups=mesh['member'=2,'grid'=16] {'member','grid'}, use_global_device_ids=true, to_apply=%region_2.3 | all-reduce | flops 12288 | bytes 98304 | tf_op jit(solution)/shard_map/psum | solution.py:306
  136.4 1.2 slice_bitcast_fusion
  137.6 16.2 %reduce-scatter.2.cloned.1.call-done = f32[32,512]{1,0:T(8,128)} async-done(((f32[512,512]{1,0:T(8,128)}), f32[32,512]{1,0:T(8,128)}) %reduce-scatter.2.cloned.1.call-update) | async-done | bytes 65552 | tf_op jit(solution)/shard_map/reduce_scatter | solution.py:311
  153.8 0.0 all-reduce.2.cloned.1.call-update
  153.8 0.6 slice_reduce_fusion.1
  154.5 21.5 %all-reduce.2.cloned.1.call-done = f32[32,512]{1,0:T(8,128)} async-done(((f32[32,512]{1,0:T(8,128)}), f32[32,512]{1,0:T(8,128)}) %all-reduce.2.cloned.1.call-update) | async-done | bytes 65552 | tf_op jit(solution)/shard_map/psum | solution.py:310
  175.9 1.5 copy.16
Async XLA Ops:
  7.2 146.6 %reduce-scatter.2.cloned.1.call-start = ((), (), s32[]{:S(2)}) async-start(), calls=%async_computation.1 | async-start | bytes 1114112 | tf_op jit(solution)/shard_map/reduce_scatter | solution.py:311
  95.9 80.0 %all-reduce.2.cloned.1.call-start = ((), (), s32[]{:S(2)}) async-start(), calls=%async_computation.2 | async-start | bytes 131072 | tf_op jit(solution)/shard_map/psum | solution.py:310
Sparse Core Ops, SparseCore 0:
  96.0 57.7 reduce-scatter.1
  156.1 19.7 all-reduce.1

commit v2 on v1

--- a/solution.py
+++ b/solution.py
@@ -57,8 +57,32 @@
     out_acc,
     send_sem,
     recv_sem,
+    grad_acc,
+    small_acc,
+    b_out_col,
+    pair_grad_in,
+    pair_small_in,
+    pair_sum,
+    group_grad,
+    group_small,
+    group_sum,
+    chip_grad,
+    chip_small,
+    final_grad,
+    final_small,
+    red_send,
+    red_recv,
 ):
     step = pl.program_id(0)
+    grid_me = lax.axis_index("grid")
+    core = lax.rem(grid_me, 2)
+    chip = grid_me // 2
+    chips = grad_acc.shape[0]
+    block_rows = grad_acc.shape[2]
+    row_parts = min(groups, block_rows // 8)
+    col_parts = groups // row_parts
+    part_rows = block_rows // row_parts
+    part_cols = grad_acc.shape[3] // col_parts
     me = lax.axis_index("member")
     mem_dev, tile, in_width = lat_ref.shape
     width = w_in_ref.shape[1]
@@ -134,7 +158,7 @@
         outs = lax.dot_general(
             w_out_t_ref[...], hid_block, (((1,), (1,)), ((), ())), preferred_element_type=jnp.float32
         )
-        squash = jnp.tanh(outs + b_out_ref[...])
+        squash = jnp.tanh(outs + jnp.tile(b_out_col[...], (1, chunk_rows // 128)))
         for m in range(mem_chunk):
             part = squash[:, m * tile : (m + 1) * tile]
             place = pl.ds((first + m) * nvars, nvars)
@@ -173,29 +197,111 @@
             for copy in copies(step):
                 copy.start()
         if do_backward:
-            small_ref[0:nvars, :] += jnp.dot(
+            small_acc[0] += jnp.dot(
                 grads_b, hid_buf[late_slot], preferred_element_type=jnp.float32
             )
-            grad_ref[...] += lax.dot_general(
+            grad_acc[...] += lax.dot_general(
                 late_ref[...].reshape(rows, in_width),
                 pre_buf[...],
                 (((0,), (0,)), ((), ())),
                 preferred_element_type=jnp.float32,
+            ).reshape(grad_acc.shape)
+
+    def member_id(hop):
+        return {"member": lax.rem(me + hop, groups)}
+
+    def core_id():
+        return {"grid": chip * 2 + 1 - core}
+
+    def chip_id(hop):
+        return {"grid": lax.rem(chip + hop, chips) * 2 + core}
+
+    def send(number, source, target, device):
+        copy = pltpu.make_async_remote_copy(
+            src_ref=source,
+            dst_ref=target,
+            send_sem=red_send.at[number],
+            recv_sem=red_recv.at[number],
+            device_id=device,
+            device_id_type=pl.DeviceIdType.MESH,
+        )
+        copy.start()
+        return copy
+
+    def part_of(member):
+        first_row = pl.multiple_of(lax.rem(member, row_parts) * part_rows, part_rows)
+        first_col = pl.multiple_of((member // row_parts) * part_cols, part_cols)
+        return pl.ds(first_row, part_rows), pl.ds(first_col, part_cols)
+
+    def reduce_gradients():
+        number = 0
+        waits = [
+            send(0, small_acc.at[1 - core], pair_small_in, core_id()),
+            send(1, grad_acc.at[:, 1 - core], pair_grad_in, core_id()),
+        ]
+        number = 2
+        for copy in waits:
+            copy.wait()
+        pair_sum[...] = grad_acc[:, core] + pair_grad_in[...]
+        group_small[0] = small_acc[core] + pair_small_in[...]
+        waits = []
+        for hop in range(1, groups):
+            rows_at, cols_at = part_of(lax.rem(me + hop, groups))
+            waits.append(send(number, group_small.at[0], group_small.at[hop], member_id(hop)))
+            waits.append(
+                send(number + 1, pair_sum.at[:, rows_at, cols_at], group_grad.at[hop], member_id(hop))
             )
+            number += 2
+        rows_at, cols_at = part_of(me)
+        group_grad[0] = pair_sum[:, rows_at, cols_at]
+        for copy in waits:
+            copy.wait()
+
+        def in_order(ref, own, count):
+            total = ref[own]
+            for index in range(1, count):
+                total = total + ref[lax.rem(own - index + count, count)]
+            return total
+
+        group_sum[...] = in_order(group_grad, me, groups)
+        chip_small[0] = in_order(group_small, me, groups)
+        chip_grad[0] = group_sum[chip]
+        waits = []
+        for hop in range(1, chips):
+            target = lax.rem(chip + hop, chips)
+            waits.append(send(number, group_sum.at[target], chip_grad.at[hop], chip_id(hop)))
+            waits.append(send(number + 1, chip_small.at[0], chip_small.at[hop], chip_id(hop)))
+            number += 2
+        for copy in waits:
+            copy.wait()
+        final_grad[rows_at, cols_at] = in_order(chip_grad, chip, chips)
+        final_small[core] = in_order(chip_small, chip, chips)
+        waits = [send(number, final_small.at[core], final_small.at[core], core_id())]
+        number += 1
+        for hop in range(1, groups):
+            piece = final_grad.at[rows_at, cols_at]
+            waits.append(send(number, piece, piece, member_id(hop)))
+            number += 1
+        for copy in waits:
+            copy.wait()
+        grad_ref[...] = final_grad[...]
+        small_ref[...] = final_small[...].reshape(small_ref.shape)
 
     @pl.when(step == 0)
     def _():
         barrier = pltpu.get_barrier_semaphore()
-        for hop in range(1, groups):
-            pl.semaphore_signal(
-                barrier,
-                inc=1,
-                device_id={"member": lax.rem(me + hop, groups)},
-                device_id_type=pl.DeviceIdType.MESH,
-            )
-        pl.semaphore_wait(barrier, groups - 1)
-        grad_ref[...] = jnp.zeros_like(grad_ref)
-        small_ref[...] = jnp.zeros_like(small_ref)
+        peers = [member_id(hop) for hop in range(1, groups)] + [core_id()]
+        peers += [chip_id(hop) for hop in range(1, chips)]
+        for peer in peers:
+            pl.semaphore_signal(barrier, inc=1, device_id=peer, device_id_type=pl.DeviceIdType.MESH)
+        pl.semaphore_wait(barrier, len(peers))
+        variable = lax.broadcasted_iota(jnp.int32, b_out_col.shape, 0)
+        column = jnp.zeros(b_out_col.shape, jnp.float32)
+        for index in range(nvars):
+            column = jnp.where(variable == index, b_out_ref[index], column)
+        b_out_col[...] = column
+        grad_acc[...] = jnp.zeros_like(grad_acc)
+        small_acc[...] = jnp.zeros_like(small_acc)
         bias_acc[...] = jnp.zeros_like(bias_acc)
         out_acc[...] = jnp.zeros_like(out_acc)
 
@@ -213,10 +319,13 @@
 
     @pl.when(step == tiles + LAG - 1)
     def _():
-        small_ref[nvars : nvars + 8, :] = bias_acc[...]
-        small_ref[nvars + 8 : 2 * nvars + 8, :] = jnp.broadcast_to(
-            jnp.sum(out_acc[...], axis=1, keepdims=True), (nvars, width)
-        )
+        sums = jnp.sum(out_acc[...], axis=1, keepdims=True)
+        line = lax.broadcasted_iota(jnp.int32, (nvars, width), 0)
+        lane = lax.broadcasted_iota(jnp.int32, (nvars, width), 1)
+        spread = jnp.sum(jnp.where(line == lane, sums, 0.0), axis=0, keepdims=True)
+        bias = jnp.sum(bias_acc[...], axis=0, keepdims=True)
+        small_acc[1] = jnp.where(line == 0, bias, jnp.where(line == 1, spread, 0.0))
+        reduce_gradients()
 
 
 def shards(
@@ -239,6 +348,13 @@
     loss_scale = 2.0 / math.sqrt(all_cells * members)
     tiles = cell_count // TILE
     rows = mem_dev * TILE
+    shards_grid = lax.axis_size("grid")
+    chips = shards_grid // 2
+    block_rows = in_width // shards_grid
+    row_parts = min(groups, block_rows // 8)
+    part_rows = block_rows // row_parts
+    part_cols = width // (groups // row_parts)
+    copies = 3 + 3 * (groups - 1) + 2 * (chips - 1)
     first_cell = lax.axis_index("grid") * cell_count
     area = area_weights(first_cell, cell_count)
     weights = (var_weight[:, None] * area[None, :]) * loss_scale
@@ -253,7 +369,7 @@
         return pl.BlockSpec(shape, lambda step: (0,) * len(shape))
 
     cell_spec = pl.BlockSpec((nvars, TILE), lambda step: (0, late(step)))
-    local_grad, small = pl.pallas_call(
+    grad_shard, small = pl.pallas_call(
         functools.partial(fused_kernel, groups, tiles),
         grid=(tiles + LAG,),
         in_specs=[
@@ -262,16 +378,16 @@
             whole(in_width, width),
             whole(1, width),
             whole(nvars, width),
-            whole(nvars, 1),
+            pl.BlockSpec(memory_space=pltpu.SMEM),
             pl.BlockSpec((mem_dev, nvars, TILE), lambda step: (0, 0, now(step))),
             cell_spec,
             cell_spec,
             cell_spec,
         ],
-        out_specs=[whole(in_width, width), whole(2 * nvars + 8, width)],
+        out_specs=[whole(block_rows, width), whole(2 * nvars, width)],
         out_shape=[
-            jax.ShapeDtypeStruct((in_width, width), jnp.float32),
-            jax.ShapeDtypeStruct((2 * nvars + 8, width), jnp.float32),
+            jax.ShapeDtypeStruct((block_rows, width), jnp.float32),
+            jax.ShapeDtypeStruct((2 * nvars, width), jnp.float32),
         ],
         scratch_shapes=[
             pltpu.VMEM((LAG + 1, rows, width), jnp.bfloat16),
@@ -284,6 +400,21 @@
             pltpu.VMEM((nvars, TILE), jnp.float32),
             pltpu.SemaphoreType.DMA((groups - 1, tiles)),
             pltpu.SemaphoreType.DMA((groups - 1, tiles)),
+            pltpu.VMEM((chips, 2, block_rows, width), jnp.float32),
+            pltpu.VMEM((2, nvars, width), jnp.float32),
+            pltpu.VMEM((nvars, 128), jnp.float32),
+            pltpu.VMEM((chips, block_rows, width), jnp.float32),
+            pltpu.VMEM((nvars, width), jnp.float32),
+            pltpu.VMEM((chips, block_rows, width), jnp.float32),
+            pltpu.VMEM((groups, chips, part_rows, part_cols), jnp.float32),
+            pltpu.VMEM((groups, nvars, width), jnp.float32),
+            pltpu.VMEM((chips, part_rows, part_cols), jnp.float32),
+            pltpu.VMEM((chips, part_rows, part_cols), jnp.float32),
+            pltpu.VMEM((chips, nvars, width), jnp.float32),
+            pltpu.VMEM((block_rows, width), jnp.float32),
+            pltpu.VMEM((2, nvars, width), jnp.float32),
+            pltpu.SemaphoreType.DMA((copies,)),
+            pltpu.SemaphoreType.DMA((copies,)),
         ],
         compiler_params=pltpu.CompilerParams(
             collective_id=0,
@@ -297,18 +428,15 @@
         weight_in,
         bias_in.reshape(1, -1),
         weight_out.T,
-        bias_out.reshape(-1, 1),
+        bias_out,
         member_rank,
         target_level,
         target_jitter,
         weights,
     )
-    total = lax.psum(small, ("member", "grid"))
-    grad_w_out = total[:nvars].T
-    grad_b_in = jnp.sum(total[nvars : nvars + 8], axis=0)
-    grad_b_out = total[nvars + 8 :, 0]
-    summed = lax.psum(local_grad, "member")
-    grad_shard = lax.psum_scatter(summed, "grid", scatter_dimension=0, tiled=True)
+    grad_w_out = small[:nvars].T
+    grad_b_in = small[nvars]
+    grad_b_out = small[nvars + 1, :nvars]
     return (grad_shard, grad_b_in, grad_w_out, grad_b_out)
 
 

time: 185 us -> 116 us (0.63)
  blocking collectives: 40.4 us -> 0 us
  waiting for transfers between devices: 37.7 us -> 0 us
  Pallas kernels: 85.9 us -> 108 us
  between operations: 14.1 us -> 0.65 us
  local copies, waits for them, and re-layouts: 3.42 us -> 5.28 us
    psum x1 -> x0, blocking collectives: 40.4 us -> none  [shards(): total = lax.psum(small, ('member', 'grid'))]
    pallas_call x1, Pallas kernels: 85.9 us -> 108 us  [shards(): pl.pallas_call(functools.partial(fused_kernel, groups, tiles), grid=(tile...]
    psum x1 -> x0, waiting for transfers between devices: 21.5 us -> none  [shards(): summed = lax.psum(local_grad, 'member')]
    reduce_scatter x1 -> x0, waiting for transfers between devices: 16.2 us -> none  [shards(): lax.psum_scatter(summed, 'grid', scatter_dimension=0, tiled=True)]
  transfers between devices with their start and end apart: 2 -> 0, of which waited for: 2 -> 0; matrix products, arithmetic and copies ran while one was open for 1% -> 0% of each run, Pallas kernels for 0% -> 0%
where the time goes in v2:
time: 116 us
  Pallas kernels  108 us (93%)
  local copies, waits for them, and re-layouts  5.28 us (5%)
  other arithmetic  1.44 us (1%)
    pallas_call x1, Pallas kernels, shards(): pl.pallas_call(functools.partial(fused_kernel, groups, tiles), grid=(tile...  108 us

profile of v2, /device:TPU:0, one launch (start us, length us, event | category | flops | bytes accessed | tf_op | source)
XLA Modules:
  0.0 115.8 jit_solution(10954446630432777732)
XLA Ops:
  0.6 0.1 fusion.5
  0.7 1.4 %multiply_multiply_fusion.weight_ref = f32[8,3072]{1,0:T(8,128)} fusion(f32[3072]{0:T(1024)S(1)} %fusion.5, f32[8]{0:T(128)} %param.17), kind=kLoop, calls=%fused_computation | loop fusion | flops 49152 | bytes 110624 | tf_op jit(solution)/shard_map/mul | solution.py:360
  2.1 108.4 %shard_map.120 = (f32[32,512]{1,0:T(8,128)}, f32[16,512]{1,0:T(8,128)}) custom-call(bf16[8,3072,512]{2,1,0:T(8,128)(2,1)} %late_ref.1, bf16[8,3072,512]{2,1,0:T(8,128)(2,1)} %late_ref.1, bf16[512,512]{1,0:T(8,128)(2,1)} %w_in_ref.1, f32[1,512]{1,0:T(1,128)} %bitcast.9, bf16[8,512]{1,0:T(8,128)(2,1)} %bitcast.7, f32[8]{0:T(128)} %b_out_ref.1, ...), custom_call_target="tpu_custom_call" | custom-call | tf_op jit(solution)/shard_map/pallas_call | solution.py:372
  110.5 1.2 %slice_bitcast_fusion.1 = f32[8]{0:T(128)} fusion(f32[16,512]{1,0:T(8,128)} %get-tuple-element.7), kind=kLoop, calls=%fused_computation.13 | loop fusion | bytes 64 | tf_op jit(solution)/shard_map/squeeze | solution.py:439
  111.7 1.3 %slice.9 = f32[1,512]{1,0:T(1,128)} slice(f32[16,512]{1,0:T(8,128)} %get-tuple-element.7), slice={[8:9], [0:512]} | slice | bytes 4096 | tf_op jit(solution)/shard_map/slice | solution.py:438
  113.0 1.3 %slice_bitcast_fusion = f32[512,8]{0,1:T(8,128)} fusion(f32[16,512]{1,0:T(8,128)} %get-tuple-element.7), kind=kLoop, calls=%fused_computation.2 | loop fusion | bytes 32768 | tf_op jit(solution)/shard_map/transpose | solution.py:437
  114.3 1.5 %copy.14 = f32[32,512]{1,0:T(8,128)} copy(f32[32,512]{1,0:T(8,128)} %get-tuple-element.12) | data formatting | bytes 131072

commit v3 on v2

--- a/solution.py
+++ b/solution.py
@@ -10,8 +10,8 @@
 
 LONS = 1440
 LAG = 2
-TILE = 128
-CHUNK_ROWS = 256
+TILE = 256
+CHUNK_ROWS = 512
 SUB_ROWS = 32
 
 north_row = 200.0
@@ -21,13 +21,6 @@
 cube_coef = 0.044715
 
 
-def area_weights(first_cell, count):
-    global_cell = first_cell + jnp.arange(count, dtype=jnp.int32)
-    lat_row = (global_cell // LONS).astype(jnp.float32)
-    latitude = (90.0 - 0.25 * (north_row + lat_row)) * (math.pi / 180.0)
-    return jnp.cos(latitude)
-
-
 def soft_sign(values):
     return values * lax.rsqrt(values * values + smooth_square)
 
@@ -35,6 +28,7 @@
 def fused_kernel(
     groups,
     tiles,
+    loss_scale,
     lat_ref,
     late_ref,
     w_in_ref,
@@ -60,6 +54,7 @@
     grad_acc,
     small_acc,
     b_out_col,
+    weight_col,
     pair_grad_in,
     pair_small_in,
     pair_sum,
@@ -89,7 +84,7 @@
     nvars = w_out_t_ref.shape[0]
     rows = mem_dev * tile
     members = mem_dev * groups
-    mem_chunk = max(1, CHUNK_ROWS // tile)
+    mem_chunk = min(mem_dev, max(1, CHUNK_ROWS // tile))
     chunk_rows = mem_chunk * tile
 
     def copies(index):
@@ -119,7 +114,10 @@
         for value in own[1:] + other:
             center = center + value
         pull = (2.0 * mean_weight) * (center * (1.0 / members) - target)
-        weight = weight_ref[...]
+        cell = grid_me * (tiles * tile) + index * tile + lax.broadcasted_iota(jnp.int32, (nvars, tile), 1)
+        lat_row = jnp.floor((cell.astype(jnp.float32) + 0.5) * (1.0 / LONS))
+        latitude = (90.0 - 0.25 * (north_row + lat_row)) * (math.pi / 180.0)
+        weight = jnp.cos(latitude) * jnp.tile(weight_col[...], (1, tile // 128))
         pair = [jnp.zeros_like(target) for _ in range(mem_dev)]
         for a in range(mem_dev):
             for b in range(a + 1, mem_dev):
@@ -234,48 +232,60 @@
         return pl.ds(first_row, part_rows), pl.ds(first_col, part_cols)
 
     def reduce_gradients():
-        number = 0
-        waits = [
-            send(0, small_acc.at[1 - core], pair_small_in, core_id()),
-            send(1, grad_acc.at[:, 1 - core], pair_grad_in, core_id()),
+        def in_order(read, own, count):
+            total = read(own)
+            for index in range(1, count):
+                total = total + read(lax.rem(own - index + count, count))
+            return total
+
+        order = [lax.rem(chip + hop, chips) for hop in range(1, chips + 1)]
+        rows_at, cols_at = part_of(me)
+        small_pair = send(0, small_acc.at[1 - core], pair_small_in, core_id())
+        pairs = [
+            send(1 + at, grad_acc.at[block, 1 - core], pair_grad_in.at[block], core_id())
+            for at, block in enumerate(order)
         ]
-        number = 2
-        for copy in waits:
+        number = 1 + chips
+        small_pair.wait()
+        group_small[0] = small_acc[core] + pair_small_in[...]
+        small_group = []
+        for hop in range(1, groups):
+            small_group.append(send(number, group_small.at[0], group_small.at[hop], member_id(hop)))
+            number += 1
+        members_waits = []
+        for at, block in enumerate(order):
+            pairs[at].wait()
+            pair_sum[block] = grad_acc[block, core] + pair_grad_in[block]
+            waits = []
+            for hop in range(1, groups):
+                rows_to, cols_to = part_of(lax.rem(me + hop, groups))
+                piece = pair_sum.at[block, rows_to, cols_to]
+                waits.append(send(number, piece, group_grad.at[hop, block], member_id(hop)))
+                number += 1
+            group_grad[0, block] = pair_sum[block, rows_at, cols_at]
+            members_waits.append(waits)
+        for copy in small_group:
             copy.wait()
-        pair_sum[...] = grad_acc[:, core] + pair_grad_in[...]
-        group_small[0] = small_acc[core] + pair_small_in[...]
-        waits = []
-        for hop in range(1, groups):
-            rows_at, cols_at = part_of(lax.rem(me + hop, groups))
-            waits.append(send(number, group_small.at[0], group_small.at[hop], member_id(hop)))
-            waits.append(
-                send(number + 1, pair_sum.at[:, rows_at, cols_at], group_grad.at[hop], member_id(hop))
-            )
-            number += 2
-        rows_at, cols_at = part_of(me)
-        group_grad[0] = pair_sum[:, rows_at, cols_at]
-        for copy in waits:
+        chip_small[0] = in_order(lambda slot: group_small[slot], me, groups)
+        chip_waits = []
+        for hop in range(1, chips):
+            chip_waits.append(send(number, chip_small.at[0], chip_small.at[hop], chip_id(hop)))
+            number += 1
+        for at, block in enumerate(order):
+            for copy in members_waits[at]:
+                copy.wait()
+            group_sum[block] = in_order(lambda slot: group_grad[slot, block], me, groups)
+            if at < chips - 1:
+                chip_waits.append(
+                    send(number, group_sum.at[block], chip_grad.at[at + 1], chip_id(at + 1))
+                )
+                number += 1
+            else:
+                chip_grad[0] = group_sum[block]
+        for copy in chip_waits:
             copy.wait()
-
-        def in_order(ref, own, count):
-            total = ref[own]
-            for index in range(1, count):
-                total = total + ref[lax.rem(own - index + count, count)]
-            return total
-
-        group_sum[...] = in_order(group_grad, me, groups)
-        chip_small[0] = in_order(group_small, me, groups)
-        chip_grad[0] = group_sum[chip]
-        waits = []
-        for hop in range(1, chips):
-            target = lax.rem(chip + hop, chips)
-            waits.append(send(number, group_sum.at[target], chip_grad.at[hop], chip_id(hop)))
-            waits.append(send(number + 1, chip_small.at[0], chip_small.at[hop], chip_id(hop)))
-            number += 2
-        for copy in waits:
-            copy.wait()
-        final_grad[rows_at, cols_at] = in_order(chip_grad, chip, chips)
-        final_small[core] = in_order(chip_small, chip, chips)
+        final_grad[rows_at, cols_at] = in_order(lambda slot: chip_grad[slot], chip, chips)
+        final_small[core] = in_order(lambda slot: chip_small[slot], chip, chips)
         waits = [send(number, final_small.at[core], final_small.at[core], core_id())]
         number += 1
         for hop in range(1, groups):
@@ -300,6 +310,9 @@
         for index in range(nvars):
             column = jnp.where(variable == index, b_out_ref[index], column)
         b_out_col[...] = column
+        for index in range(nvars):
+            column = jnp.where(variable == index, weight_ref[index] * loss_scale, column)
+        weight_col[...] = column
         grad_acc[...] = jnp.zeros_like(grad_acc)
         small_acc[...] = jnp.zeros_like(small_acc)
         bias_acc[...] = jnp.zeros_like(bias_acc)
@@ -326,6 +339,14 @@
         bias = jnp.sum(bias_acc[...], axis=0, keepdims=True)
         small_acc[1] = jnp.where(line == 0, bias, jnp.where(line == 1, spread, 0.0))
         reduce_gradients()
+
+
+def split_kernel(grad_ref, small_ref, grad_out, b_in_out, w_out_t_out, b_out_out):
+    nvars = w_out_t_out.shape[0]
+    grad_out[...] = grad_ref[...]
+    w_out_t_out[...] = small_ref[0:nvars, :]
+    b_in_out[...] = small_ref[nvars : nvars + 1, :]
+    b_out_out[...] = small_ref[nvars + 1 : nvars + 2, 0:nvars]
 
 
 def shards(
@@ -354,10 +375,7 @@
     row_parts = min(groups, block_rows // 8)
     part_rows = block_rows // row_parts
     part_cols = width // (groups // row_parts)
-    copies = 3 + 3 * (groups - 1) + 2 * (chips - 1)
-    first_cell = lax.axis_index("grid") * cell_count
-    area = area_weights(first_cell, cell_count)
-    weights = (var_weight[:, None] * area[None, :]) * loss_scale
+    copies = chips * (groups + 2) + 2 * groups
 
     def now(step):
         return jnp.minimum(step, tiles - 1)
@@ -370,7 +388,7 @@
 
     cell_spec = pl.BlockSpec((nvars, TILE), lambda step: (0, late(step)))
     grad_shard, small = pl.pallas_call(
-        functools.partial(fused_kernel, groups, tiles),
+        functools.partial(fused_kernel, groups, tiles, loss_scale),
         grid=(tiles + LAG,),
         in_specs=[
             pl.BlockSpec((mem_dev, TILE, in_width), lambda step: (0, now(step), 0)),
@@ -382,7 +400,7 @@
             pl.BlockSpec((mem_dev, nvars, TILE), lambda step: (0, 0, now(step))),
             cell_spec,
             cell_spec,
-            cell_spec,
+            pl.BlockSpec(memory_space=pltpu.SMEM),
         ],
         out_specs=[whole(block_rows, width), whole(2 * nvars, width)],
         out_shape=[
@@ -402,6 +420,7 @@
             pltpu.SemaphoreType.DMA((groups - 1, tiles)),
             pltpu.VMEM((chips, 2, block_rows, width), jnp.float32),
             pltpu.VMEM((2, nvars, width), jnp.float32),
+            pltpu.VMEM((nvars, 128), jnp.float32),
             pltpu.VMEM((nvars, 128), jnp.float32),
             pltpu.VMEM((chips, block_rows, width), jnp.float32),
             pltpu.VMEM((nvars, width), jnp.float32),
@@ -432,11 +451,20 @@
         member_rank,
         target_level,
         target_jitter,
-        weights,
+        var_weight,
     )
-    grad_w_out = small[:nvars].T
-    grad_b_in = small[nvars]
-    grad_b_out = small[nvars + 1, :nvars]
+    grad_shard, grad_b_in, grad_w_out_t, grad_b_out = pl.pallas_call(
+        split_kernel,
+        out_shape=[
+            jax.ShapeDtypeStruct((block_rows, width), jnp.float32),
+            jax.ShapeDtypeStruct((1, width), jnp.float32),
+            jax.ShapeDtypeStruct((nvars, width), jnp.float32),
+            jax.ShapeDtypeStruct((1, nvars), jnp.float32),
+        ],
+    )(grad_shard, small)
+    grad_b_in = grad_b_in.reshape(width)
+    grad_w_out = grad_w_out_t.T
+    grad_b_out = grad_b_out.reshape(nvars)
     return (grad_shard, grad_b_in, grad_w_out, grad_b_out)
 
 

time: 116 us -> 96 us (0.83)
  Pallas kernels: 108 us -> 95.2 us
  local copies, waits for them, and re-layouts: 5.28 us -> 0 us
  other arithmetic: 1.44 us -> 0 us
    pallas_call x1 -> x2, Pallas kernels: 108 us -> 95.2 us  [the longest x1 93.7 us: shards(): pl.pallas_call(functools.partial(fused_kernel, groups, tiles, loss_scale)...]
    unnamed x1 -> x0, local copies, waits for them, and re-layouts: 1.47 us -> none
    mul x1 -> x0, other arithmetic: 1.37 us -> none  [shards(): weights = var_weight[:, None] * area[None, :] * loss_scale]
    transpose x1 -> x0, local copies, waits for them, and re-layouts: 1.32 us -> none  [shards(): grad_w_out = small[:nvars].T]
    slice x1 -> x0, local copies, waits for them, and re-layouts: 1.3 us -> none  [shards(): grad_b_in = small[nvars]]
    squeeze x1 -> x0, local copies, waits for them, and re-layouts: 1.19 us -> none  [shards(): grad_b_out = small[nvars + 1, :nvars]]
where the time goes in v3:
time: 96 us; the launch traced here: 95.9 us
  Pallas kernels  95.2 us (99%)
    pallas_call x1, Pallas kernels, shards(): pl.pallas_call(functools.partial(fused_kernel, groups, tiles, loss_scale)...  93.7 us

profile of v3, /device:TPU:0, one launch (start us, length us, event | category | flops | bytes accessed | tf_op | source)
XLA Modules:
  0.0 95.9 jit_solution(1795146165449235707)
XLA Ops:
  0.6 93.7 %shard_map.120 = (f32[32,512]{1,0:T(8,128)}, f32[16,512]{1,0:T(8,128)}) custom-call(bf16[8,3072,512]{2,1,0:T(8,128)(2,1)} %late_ref.1, bf16[8,3072,512]{2,1,0:T(8,128)(2,1)} %late_ref.1, bf16[512,512]{1,0:T(8,128)(2,1)} %w_in_ref.1, f32[1,512]{1,0:T(1,128)} %bitcast.6, bf16[8,512]{1,0:T(8,128)(2,1)} %bitcast.5, f32[8]{0:T(128)} %b_out_ref.1, ...), custom_call_target="tpu_custom_call" | custom-call | tf_op jit(solution)/shard_map/pallas_call | solution.py:390
  94.4 1.5 %shard_map.121 = (f32[32,512]{1,0:T(8,128)}, f32[1,512]{1,0:T(1,128)}, f32[8,512]{1,0:T(8,128)}, f32[1,8]{1,0:T(1,128)}) custom-call(f32[32,512]{1,0:T(8,128)} %get-tuple-element.10.grad_ref, f32[16,512]{1,0:T(8,128)} %get-tuple-element.11.small_ref), custom_call_target="tpu_custom_call" | custom-call | tf_op jit(solution)/shard_map/pallas_call | solution.py:456
